TPU v7x, 32 devices: a whole 2x2x4 slice. The times are simulated.
32 devices in a mesh: groups: 2 (over y), res: 16 (over z, x, core).
Axes of the slice: x: 2, y: 2, z: 4, core: 2. Of those that a mesh axis runs over, the one named last changes fastest.
Arguments:
- homolog_embedding: bfloat16 [512, 64, 256], P('groups', 'res'), parts along dimension 0, may hold values from -6 to 6
- pair_state: bfloat16 [128, 64, 128], P(('groups', 'res')), parts along dimension 0, may hold values from -6 to 6
- homolog_norm_scale: float32 [256], replicated, may hold values from 0.25 to 1.75
- former_operand_matrix: bfloat16 [256, 32], replicated, may hold values from -0.375 to 0.375
- latter_operand_matrix: bfloat16 [256, 32], replicated, may hold values from -0.375 to 0.375
- outer_mean_weight: bfloat16 [1024, 128], replicated, may hold values from -0.1875 to 0.1875
- outer_mean_bias: float32 [128], replicated, may hold values from -3 to 3
- outgoing_input_gain: float32 [128], replicated, may hold values from 0.25 to 1.75
- outgoing_edge_weight: bfloat16 [128, 256], replicated, may hold values from -0.5 to 0.5
- outgoing_gate_weight: bfloat16 [128, 128], replicated, may hold values from -0.5 to 0.5
- outgoing_product_gain: float32 [64], replicated, may hold values from 0.25 to 1.75
- outgoing_output_weight: bfloat16 [64, 128], replicated, may hold values from -0.75 to 0.75
- incoming_input_gain: float32 [128], replicated, may hold values from 0.25 to 1.75
- incoming_edge_weight: bfloat16 [128, 256], replicated, may hold values from -0.5 to 0.5
- incoming_gate_weight: bfloat16 [128, 128], replicated, may hold values from -0.5 to 0.5
- incoming_product_gain: float32 [64], replicated, may hold values from 0.25 to 1.75
- incoming_output_weight: bfloat16 [64, 128], replicated, may hold values from -0.75 to 0.75
Outputs:
- pair_three: bfloat16 [128, 64, 128], P(('groups', 'res')), parts along dimension 0
There are 2 independent parts, one for each index of `groups`. A program takes and returns all parts, laid end to end along the dimension named above; an argument that names none is the same for every part. Nothing has to cross between parts.
All inputs are finite; a program needn't handle non-finite values.
Results may differ from a plain program's by a relative error of at most 0.013.
Values may be sent and summed in bfloat16 or wider, within the bound.
A program may use at most 128 MiB of HBM per device.

v0:
```python
import jax
import jax.numpy as jnp
from jax import lax
from jax.sharding import PartitionSpec as P


def layer_normalize(values, gain):
    mean_val = jnp.mean(values, axis=-1, keepdims=True)
    centred = values - mean_val
    variance = jnp.mean(centred * centred, axis=-1, keepdims=True)
    return centred / jnp.sqrt(variance + 1e-05) * gain


def project_in(pair_block, norm_gain, weight_in, weight_gate):
    hidden_width = weight_in.shape[1] // 4
    normed = layer_normalize(pair_block.astype(jnp.float32), norm_gain).astype(jnp.bfloat16)
    projected = jnp.einsum("abc,cd->abd", normed, weight_in, preferred_element_type=jnp.float32)
    edge_left = (
        jax.nn.sigmoid(projected[..., hidden_width : 2 * hidden_width])
        * projected[..., :hidden_width]
    ).astype(jnp.bfloat16)
    edge_right = (
        jax.nn.sigmoid(projected[..., 3 * hidden_width :])
        * projected[..., 2 * hidden_width : 3 * hidden_width]
    ).astype(jnp.bfloat16)
    gating = jax.nn.sigmoid(
        jnp.einsum("abc,cd->abd", normed, weight_gate, preferred_element_type=jnp.float32)
    )
    return (edge_left, edge_right, gating)


def apply_update(pair_block, gating, mixed_normed, weight_final):
    update = jnp.einsum(
        "abc,cd->abd", mixed_normed, weight_final, preferred_element_type=jnp.float32
    )
    return (pair_block.astype(jnp.float32) + gating * update).astype(jnp.bfloat16)


def shards(
    homolog_embedding,
    pair_state,
    homolog_norm_scale,
    former_operand_matrix,
    latter_operand_matrix,
    outer_mean_weight,
    outer_mean_bias,
    outgoing_input_gain,
    outgoing_edge_weight,
    outgoing_gate_weight,
    outgoing_product_gain,
    outgoing_output_weight,
    incoming_input_gain,
    incoming_edge_weight,
    incoming_gate_weight,
    incoming_product_gain,
    incoming_output_weight,
):
    sequence_rows = homolog_embedding.shape[0]
    alignment_normalized = layer_normalize(
        homolog_embedding.astype(jnp.float32), homolog_norm_scale
    ).astype(jnp.bfloat16)
    left_factor = jnp.einsum(
        "vfd,dl->vfl",
        alignment_normalized,
        former_operand_matrix,
        preferred_element_type=jnp.float32,
    ).astype(jnp.bfloat16)
    right_factor = jnp.einsum(
        "vfd,dl->vfl",
        alignment_normalized,
        latter_operand_matrix,
        preferred_element_type=jnp.float32,
    ).astype(jnp.bfloat16)
    outer = (
        jnp.einsum(
            "sip,sjq->ijpq",
            left_factor,
            lax.all_gather(right_factor, "res", axis=1, tiled=True),
            preferred_element_type=jnp.float32,
        )
        / sequence_rows
    )
    flattened = outer.reshape(outer.shape[0], outer.shape[1], -1).astype(jnp.bfloat16)
    outer_update = (
        jnp.einsum("ijr,rc->ijc", flattened, outer_mean_weight, preferred_element_type=jnp.float32)
        + outer_mean_bias
    )
    pair_one = (pair_state.astype(jnp.float32) + outer_update).astype(jnp.bfloat16)
    edge_left, edge_right, gating = project_in(
        pair_one, outgoing_input_gain, outgoing_edge_weight, outgoing_gate_weight
    )
    mixed = jnp.einsum(
        "ikc,jkc->ijc",
        edge_left,
        lax.all_gather(edge_right, "res", axis=0, tiled=True),
        preferred_element_type=jnp.float32,
    )
    mixed_normed = layer_normalize(mixed, outgoing_product_gain).astype(jnp.bfloat16)
    pair_two = apply_update(pair_one, gating, mixed_normed, outgoing_output_weight)
    columns = lax.all_to_all(pair_two, "res", split_axis=1, concat_axis=0, tiled=True)
    col_left, col_right, col_gating = project_in(
        columns, incoming_input_gain, incoming_edge_weight, incoming_gate_weight
    )
    col_mixed = jnp.einsum(
        "kic,kjc->ijc",
        lax.all_gather(col_left, "res", axis=1, tiled=True),
        col_right,
        preferred_element_type=jnp.float32,
    )
    col_normed = layer_normalize(col_mixed, incoming_product_gain).astype(jnp.bfloat16)
    finished = apply_update(columns, col_gating, col_normed, incoming_output_weight)
    pair_three = lax.all_to_all(finished, "res", split_axis=0, concat_axis=1, tiled=True)
    return pair_three


def solution(mesh):
    in_specs = (
        P("groups", "res", None),
        P(("groups", "res"), None, None),
        P(),
        P(),
        P(),
        P(),
        P(),
        P(),
        P(),
        P(),
        P(),
        P(),
        P(),
        P(),
        P(),
        P(),
        P(),
    )
    out_specs = P(("groups", "res"), None, None)
    return jax.shard_map(shards, mesh=mesh, in_specs=in_specs, out_specs=out_specs, check_vma=False)
```

profile of v0, /device:TPU:0, one launch (start us, length us, event | category | flops | bytes accessed | tf_op | source)
XLA Modules:
  0.0 137.1 jit_solution(1992916395334262495)
XLA Ops:
  6.6 1.5 %convert_reduce_fusion = f32[256,4]{1,0:T(8,128)S(1)} fusion(bf16[256,4,256]{2,1,0:T(4,128)(2,1)} %param.17), kind=kLoop, calls=%fused_computation.3 | loop fusion | flops 523264 | bytes 528384 | tf_op jit(solution)/shard_map/reduce_sum | solution.py:8
  8.1 1.8 %fusion.21 = f32[256,4]{1,0:T(8,128)S(1)} fusion(bf16[256,4,256]{2,1,0:T(4,128)(2,1)} %param.17, f32[256,4]{1,0:T(8,128)S(1)} %broadcast_multiply_fusion), kind=kLoop, calls=%fused_computation.31 | loop fusion | flops 1047552 | bytes 532480 | tf_op jit(solution)/shard_map/reduce_sum | solution.py:10
  9.9 1.4 %fusion.20 = bf16[256,4,256]{2,1,0:T(4,128)(2,1)S(1)} fusion(bf16[256,4,256]{2,1,0:T(4,128)(2,1)S(1)} %copy-done.1, f32[256]{0:T(256)} %param.19, f32[256,4]{1,0:T(8,128)S(1)} %add_sqrt_fusion, f32[256,4]{1,0:T(8,128)S(1)} %broadcast_multiply_fusion), kind=kLoop, calls=%fused_computation.30 | loop fusion | flops 1310720 | bytes 1057792 | tf_op jit(solution)/shard_map/convert_element_type | solution.py:61
  11.3 0.9 convolution_convert_fusion.1
  12.2 40.8 %all-gather.2.cloned.1.call-done = bf16[256,64,32]{0,2,1:T(8,128)(2,1)} async-done(((bf16[256,4,32]{0,2,1:T(8,128)(2,1)}), bf16[256,64,32]{0,2,1:T(8,128)(2,1)}) %all-gather.2.cloned.1.call-update) | async-done | bytes 1048592 | tf_op jit(solution)/shard_map/all_gather | solution.py:78
  53.0 2.2 %fusion = bf16[4,64,32,32]{2,3,0,1:T(8,128)(2,1)S(1)} fusion(bf16[256,64,32]{0,2,1:T(8,128)(2,1)} %all-gather.2.cloned.1.call-done, bf16[256,4,256]{2,1,0:T(4,128)(2,1)S(1)} %fusion.20, bf16[256,32]{0,1:T(8,128)(2,1)S(1)} %copy-done.13), kind=kOutput, calls=%fused_computation.1 | convolution fusion | flops 151552000 | bytes 2113536 | tf_op jit(solution)/shard_map/sip,sjq->ijpq/dot_general | solution.py:75
  55.3 3.1 %copy.58 = bf16[4,64,32,32]{1,3,2,0:T(8,128)(2,1)S(1)} copy(bf16[4,64,32,32]{2,3,0,1:T(8,128)(2,1)S(1)} %fusion) | data formatting | bytes 1048576 | tf_op jit(solution)/shard_map/convert_element_type | solution.py:83
  58.5 0.5 fusion.60
  59.0 0.2 multiply_reduce_fusion.2
  59.2 0.3 fusion.47
  59.5 0.2 fusion.35
  59.8 22.3 %all_gather.10 = bf16[64,64,64]{2,1,0:T(8,128)(2,1)S(1)} all-gather(bf16[4,64,64]{2,1,0:T(8,128)(2,1)S(1)} %get-tuple-element.8), channel_id=1, replica_groups=mesh['groups'=2,'res'=16] {'res'}, dimensions={0}, use_global_device_ids=true | all-gather | bytes 557056 | tf_op jit(solution)/shard_map/all_gather | solution.py:95
  82.0 1.6 %copy.60 = bf16[64,64,64]{1,0,2:T(8,128)(2,1)S(1)} copy(bf16[64,64,64]{2,1,0:T(8,128)(2,1)S(1)} %all_gather.10) | data formatting | bytes 1048576 | tf_op jit(solution)/shard_map/all_gather | solution.py:95
  83.7 0.7 fusion.61
  84.5 0.1 multiply_convert_fusion.3
  84.6 0.2 fusion.51
  84.8 0.3 fusion.15
  85.2 9.5 %all_to_all.27 = bf16[4,64,128]{2,0,1:T(4,128)(2,1)S(1)} all-to-all(bf16[4,64,128]{2,0,1:T(4,128)(2,1)S(1)} %copy.63), channel_id=1, replica_groups=mesh['groups'=2,'res'=16] {'res'}, dimensions={1} | all-to-all | bytes 131072 | tf_op jit(solution)/shard_map/all_to_all | solution.py:100
  94.7 0.1 bitcast_reduce_fusion
  94.8 0.3 fusion.44
  95.1 0.2 copy.67
  95.4 0.2 copy.70
  95.8 0.3 fusion.45
  96.0 0.2 fusion.27
  96.3 20.7 %all_gather.11 = bf16[64,64,64]{2,0,1:T(8,128)(2,1)S(1)} all-gather(bf16[64,4,64]{2,0,1:T(8,128)(2,1)S(1)} %get-tuple-element.5), channel_id=1, replica_groups=mesh['groups'=2,'res'=16] {'res'}, dimensions={1}, use_global_device_ids=true | all-gather | bytes 557056 | tf_op jit(solution)/shard_map/all_gather | solution.py:106
  117.0 1.6 %copy.72 = bf16[64,64,64]{0,1,2:T(8,128)(2,1)S(1)} copy(bf16[64,64,64]{2,0,1:T(8,128)(2,1)S(1)} %all_gather.11) | data formatting | bytes 1048576 | tf_op jit(solution)/shard_map/all_gather | solution.py:106
  118.6 0.7 fusion.62
  119.4 0.1 multiply_convert_fusion.1
  119.6 0.2 fusion.49
  119.8 0.3 fusion.14
  120.1 9.5 %all_to_all.28 = bf16[64,4,128]{2,1,0:T(4,128)(2,1)S(1)} all-to-all(bf16[64,4,128]{2,1,0:T(4,128)(2,1)S(1)} %copy.74), channel_id=1, replica_groups=mesh['groups'=2,'res'=16] {'res'}, dimensions={0} | all-to-all | bytes 131072 | tf_op jit(solution)/shard_map/all_to_all | solution.py:112
  129.6 0.7 copy.75
  (54 shorter events, 1.0 us)
Async XLA Ops:
  6.5 51.9 %copy-start = (bf16[1024,128]{1,0:T(8,128)(2,1)S(1)}, bf16[1024,128]{1,0:T(8,128)(2,1)}, u32[]{:S(2)}) copy-start(bf16[1024,128]{1,0:T(8,128)(2,1)} %param.22) | copy-start | bytes 786436
  6.5 3.3 %copy-start.1 = (bf16[256,4,256]{2,1,0:T(4,128)(2,1)S(1)}, bf16[256,4,256]{2,1,0:T(4,128)(2,1)}, u32[]{:S(2)}) copy-start(bf16[256,4,256]{2,1,0:T(4,128)(2,1)} %param.17) | copy-start | bytes 1572868
  6.5 4.8 %copy-start.12 = (bf16[256,32]{0,1:T(8,128)(2,1)S(1)}, bf16[256,32]{0,1:T(8,128)(2,1)}, u32[]{:S(2)}) copy-start(bf16[256,32]{0,1:T(8,128)(2,1)} %param.21) | copy-start | bytes 49156
  6.5 46.5 %copy-start.13 = (bf16[256,32]{0,1:T(8,128)(2,1)S(1)}, bf16[256,32]{0,1:T(8,128)(2,1)}, u32[]{:S(2)}) copy-start(bf16[256,32]{0,1:T(8,128)(2,1)} %param.20) | copy-start | bytes 49156
  6.5 46.5 %all-gather.2.cloned.1.call-start = ((), (), s32[]{:S(2)}) async-start(), calls=%async_computation.2 | async-start | bytes 1114112 | tf_op jit(solution)/shard_map/all_gather | solution.py:78
  55.2 3.2 %copy-start.2 = (bf16[4,64,128]{2,1,0:T(8,128)(2,1)S(1)}, bf16[4,64,128]{2,1,0:T(8,128)(2,1)}, u32[]{:S(2)}) copy-start(bf16[4,64,128]{2,1,0:T(8,128)(2,1)} %param.18) | copy-start | bytes 196612
  55.2 3.2 %copy-start.5 = (f32[128]{0:T(128)S(1)}, f32[128]{0:T(128)}, u32[]{:S(2)}) copy-start(f32[128]{0:T(128)} %param.23) | copy-start | bytes 1540
  55.3 3.9 %copy-start.8 = (bf16[128,256]{1,0:T(8,128)(2,1)S(1)}, bf16[128,256]{1,0:T(8,128)(2,1)}, u32[]{:S(2)}) copy-start(bf16[128,256]{1,0:T(8,128)(2,1)} %param.25) | copy-start | bytes 196612
  55.3 3.9 %copy-start.14 = (f32[128]{0:T(128)S(1)}, f32[128]{0:T(128)}, u32[]{:S(2)}) copy-start(f32[128]{0:T(128)} %param.24) | copy-start | bytes 1540
  59.8 24.7 %copy-start.6 = (f32[64]{0:T(128)S(1)}, f32[64]{0:T(128)}, u32[]{:S(2)}) copy-start(f32[64]{0:T(128)} %param.27) | copy-start | bytes 772
  82.0 2.6 %copy-start.3 = (bf16[64,128]{1,0:T(8,128)(2,1)S(1)}, bf16[64,128]{1,0:T(8,128)(2,1)}, u32[]{:S(2)}) copy-start(bf16[64,128]{1,0:T(8,128)(2,1)} %param.28) | copy-start | bytes 49156
  82.0 2.8 %copy-start.10 = (bf16[128,128]{1,0:T(8,128)(2,1)S(1)}, bf16[128,128]{1,0:T(8,128)(2,1)}, u32[]{:S(2)}) copy-start(bf16[128,128]{1,0:T(8,128)(2,1)} %param.26) | copy-start | bytes 98308
  83.7 12.1 %copy-start.9 = (bf16[128,256]{1,0:T(8,128)(2,1)S(1)}, bf16[128,256]{1,0:T(8,128)(2,1)}, u32[]{:S(2)}) copy-start(bf16[128,256]{1,0:T(8,128)(2,1)} %param.30) | copy-start | bytes 196612
  83.7 12.1 %copy-start.15 = (f32[128]{0:T(128)S(1)}, f32[128]{0:T(128)}, u32[]{:S(2)}) copy-start(f32[128]{0:T(128)} %param.29) | copy-start | bytes 1540
  96.3 23.1 %copy-start.7 = (f32[64]{0:T(128)S(1)}, f32[64]{0:T(128)}, u32[]{:S(2)}) copy-start(f32[64]{0:T(128)} %param.32) | copy-start | bytes 772
  117.0 2.6 %copy-start.4 = (bf16[64,128]{1,0:T(8,128)(2,1)S(1)}, bf16[64,128]{1,0:T(8,128)(2,1)}, u32[]{:S(2)}) copy-start(bf16[64,128]{1,0:T(8,128)(2,1)} %param.33) | copy-start | bytes 49156
  117.0 2.8 %copy-start.11 = (bf16[128,128]{1,0:T(8,128)(2,1)S(1)}, bf16[128,128]{1,0:T(8,128)(2,1)}, u32[]{:S(2)}) copy-start(bf16[128,128]{1,0:T(8,128)(2,1)} %param.31) | copy-start | bytes 98308
Sparse Core Ops, SparseCore 0:
  12.4 40.6 all-gather.1
where the time goes:
time: 137 us
  blocking collectives  61.9 us (45%)
  waiting for transfers between devices  40.8 us (30%)
  between operations  13.8 us (10%)
  local copies, waits for them, and re-layouts  8.12 us (6%)
  matrix products  6.34 us (5%)
  other arithmetic  6.1 us (4%)
    all_gather x1, waiting for transfers between devices, shards(): lax.all_gather(right_factor, 'res', axis=1, tiled=True)  40.8 us
    all_gather x1, blocking collectives, shards(): lax.all_gather(edge_right, 'res', axis=0, tiled=True)  22.3 us
    all_gather x1, blocking collectives, shards(): lax.all_gather(col_left, 'res', axis=1, tiled=True)  20.7 us
    all_to_all x1, blocking collectives, shards(): lax.all_to_all(finished, 'res', split_axis=0, concat_axis=1, tiled=True)  9.51 us
    all_to_all x1, blocking collectives, shards(): lax.all_to_all(pair_two, 'res', split_axis=1, concat_axis=0, tiled=True)  9.48 us
    convert_element_type x1, local copies, waits for them, and re-layouts, shards(): outer.reshape(outer.shape[0], outer.shape[1], -1).astype(jnp.bfloat16)  3.14 us
  transfers between devices with their start and end apart: 1, of which 1 were waited for; matrix products, arithmetic and copies ran while one was open for 0% of the time, Pallas kernels for 0%

commit v1 on v0

--- a/solution.py
+++ b/solution.py
@@ -97,20 +97,17 @@
     )
     mixed_normed = layer_normalize(mixed, outgoing_product_gain).astype(jnp.bfloat16)
     pair_two = apply_update(pair_one, gating, mixed_normed, outgoing_output_weight)
-    columns = lax.all_to_all(pair_two, "res", split_axis=1, concat_axis=0, tiled=True)
-    col_left, col_right, col_gating = project_in(
-        columns, incoming_input_gain, incoming_edge_weight, incoming_gate_weight
+    in_left, in_right, in_gating = project_in(
+        pair_two, incoming_input_gain, incoming_edge_weight, incoming_gate_weight
     )
-    col_mixed = jnp.einsum(
+    in_mixed = jnp.einsum(
         "kic,kjc->ijc",
-        lax.all_gather(col_left, "res", axis=1, tiled=True),
-        col_right,
+        lax.all_to_all(in_left, "res", split_axis=1, concat_axis=0, tiled=True),
+        lax.all_gather(in_right, "res", axis=0, tiled=True),
         preferred_element_type=jnp.float32,
     )
-    col_normed = layer_normalize(col_mixed, incoming_product_gain).astype(jnp.bfloat16)
-    finished = apply_update(columns, col_gating, col_normed, incoming_output_weight)
-    pair_three = lax.all_to_all(finished, "res", split_axis=0, concat_axis=1, tiled=True)
-    return pair_three
+    in_normed = layer_normalize(in_mixed, incoming_product_gain).astype(jnp.bfloat16)
+    return apply_update(pair_two, in_gating, in_normed, incoming_output_weight)
 
 
 def solution(mesh):

time: 137 us -> 126 us (0.920)
  blocking collectives: 61.9 us -> 47 us
  starting transfers between devices: 0.03 us -> 3.53 us
    all_to_all x2 -> x0, blocking collectives: 19 us -> none  [the longest x1 9.51 us: shards(): lax.all_to_all(finished, 'res', split_axis=0, concat_axis=1, tiled=True)]
    all_gather x1, blocking collectives: 20.7 us -> 24.7 us  [shards(): lax.all_gather(in_right, 'res', axis=0, tiled=True)]
    all_to_all x0 -> x1, starting transfers between devices: none -> 3.5 us  [shards(): lax.all_to_all(in_left, 'res', split_axis=1, concat_axis=0, tiled=True)]
  transfers between devices with their start and end apart: 1 -> 2, of which waited for: 1 -> 1; matrix products, arithmetic and copies ran while one was open for 0% -> 1% of each run, Pallas kernels for 0% -> 0%
where the time goes in v1:
time: 126 us; the launch traced here: 125 us
  blocking collectives  47 us (37%)
  waiting for transfers between devices  40.8 us (32%)
  between operations  13.7 us (11%)
  local copies, waits for them, and re-layouts  7.64 us (6%)
  matrix products  6.81 us (5%)
  other arithmetic  5.86 us (5%)
  starting transfers between devices  3.53 us (3%)
    all_gather x1, waiting for transfers between devices, shards(): lax.all_gather(right_factor, 'res', axis=1, tiled=True)  40.8 us
    all_gather x1, blocking collectives, shards(): lax.all_gather(in_right, 'res', axis=0, tiled=True)  24.7 us
    all_gather x1, blocking collectives, shards(): lax.all_gather(edge_right, 'res', axis=0, tiled=True)  22.3 us
    all_to_all x1, starting transfers between devices, shards(): lax.all_to_all(in_left, 'res', split_axis=1, concat_axis=0, tiled=True)  3.5 us
    convert_element_type x1, local copies, waits for them, and re-layouts, shards(): outer.reshape(outer.shape[0], outer.shape[1], -1).astype(jnp.bfloat16)  3.14 us
  transfers between devices with their start and end apart: 2, of which 1 were waited for; matrix products, arithmetic and copies ran while one was open for 1% of the time, Pallas kernels for 0%

profile of v1, /device:TPU:0, one launch (start us, length us, event | category | flops | bytes accessed | tf_op | source)
XLA Modules:
  0.0 125.4 jit_solution(15634377013157379760)
XLA Ops:
  6.6 1.5 %convert_reduce_fusion = f32[256,4]{1,0:T(8,128)S(1)} fusion(bf16[256,4,256]{2,1,0:T(4,128)(2,1)} %param.17), kind=kLoop, calls=%fused_computation.3 | loop fusion | flops 523264 | bytes 528384 | tf_op jit(solution)/shard_map/reduce_sum | solution.py:8
  8.1 1.8 %fusion.22 = f32[256,4]{1,0:T(8,128)S(1)} fusion(bf16[256,4,256]{2,1,0:T(4,128)(2,1)} %param.17, f32[256,4]{1,0:T(8,128)S(1)} %broadcast_multiply_fusion), kind=kLoop, calls=%fused_computation.32 | loop fusion | flops 1047552 | bytes 532480 | tf_op jit(solution)/shard_map/reduce_sum | solution.py:10
  9.9 1.4 %fusion.21 = bf16[256,4,256]{2,1,0:T(4,128)(2,1)S(1)} fusion(bf16[256,4,256]{2,1,0:T(4,128)(2,1)S(1)} %copy-done.1, f32[256]{0:T(256)} %param.19, f32[256,4]{1,0:T(8,128)S(1)} %add_sqrt_fusion, f32[256,4]{1,0:T(8,128)S(1)} %broadcast_multiply_fusion), kind=kLoop, calls=%fused_computation.31 | loop fusion | flops 1310720 | bytes 1057792 | tf_op jit(solution)/shard_map/convert_element_type | solution.py:61
  11.3 0.9 convolution_convert_fusion.1
  12.2 40.8 %all-gather.2.cloned.1.call-done = bf16[256,64,32]{0,2,1:T(8,128)(2,1)} async-done(((bf16[256,4,32]{0,2,1:T(8,128)(2,1)}), bf16[256,64,32]{0,2,1:T(8,128)(2,1)}) %all-gather.2.cloned.1.call-update) | async-done | bytes 1048592 | tf_op jit(solution)/shard_map/all_gather | solution.py:78
  53.0 2.2 %fusion = bf16[4,64,32,32]{2,3,0,1:T(8,128)(2,1)S(1)} fusion(bf16[256,64,32]{0,2,1:T(8,128)(2,1)} %all-gather.2.cloned.1.call-done, bf16[256,4,256]{2,1,0:T(4,128)(2,1)S(1)} %fusion.21, bf16[256,32]{0,1:T(8,128)(2,1)S(1)} %copy-done.13), kind=kOutput, calls=%fused_computation.1 | convolution fusion | flops 151552000 | bytes 2113536 | tf_op jit(solution)/shard_map/sip,sjq->ijpq/dot_general | solution.py:75
  55.3 3.1 %copy.35 = bf16[4,64,32,32]{1,3,2,0:T(8,128)(2,1)S(1)} copy(bf16[4,64,32,32]{2,3,0,1:T(8,128)(2,1)S(1)} %fusion) | data formatting | bytes 1048576 | tf_op jit(solution)/shard_map/convert_element_type | solution.py:83
  58.5 0.5 fusion.59
  59.0 0.2 multiply_reduce_fusion.3
  59.2 0.3 fusion.46
  59.5 0.2 fusion.36
  59.6 0.1 copy.38
  59.8 22.3 %all_gather.10 = bf16[64,64,64]{2,1,0:T(8,128)(2,1)S(1)} all-gather(bf16[4,64,64]{2,1,0:T(8,128)(2,1)S(1)} %get-tuple-element.8), channel_id=1, replica_groups=mesh['groups'=2,'res'=16] {'res'}, dimensions={0}, use_global_device_ids=true | all-gather | bytes 557056 | tf_op jit(solution)/shard_map/all_gather | solution.py:95
  82.0 1.6 %copy.37 = bf16[64,64,64]{1,0,2:T(8,128)(2,1)S(1)} copy(bf16[64,64,64]{2,1,0:T(8,128)(2,1)S(1)} %all_gather.10) | data formatting | bytes 1048576 | tf_op jit(solution)/shard_map/all_gather | solution.py:95
  83.7 0.7 fusion.60
  84.3 0.1 multiply_reduce_fusion.2
  84.5 0.1 multiply_convert_fusion.3
  84.6 0.2 fusion.50
  84.8 0.4 fusion.61
  85.2 0.2 multiply_reduce_fusion.1
  85.4 0.3 fusion.44
  85.7 0.2 fusion.28
  85.9 0.7 reshape.79
  86.6 3.5 %all-to-all-start = ((bf16[16,2,512]{2,1,0:T(2,128)(2,1)}), bf16[16,2,512]{2,1,0:T(2,128)(2,1)S(1)}, u32[]{:S(2)}, u32[]{:S(2)}) async-start(bf16[16,2,512]{2,1,0:T(2,128)(2,1)} %reshape.79), calls=%async_computation | async-start | bytes 65536 | tf_op jit(solution)/shard_map/all_to_all | solution.py:105
  90.1 24.7 %all_gather.11 = bf16[64,64,64]{2,1,0:T(8,128)(2,1)S(1)} all-gather(bf16[4,64,64]{2,1,0:T(8,128)(2,1)S(1)} %get-tuple-element.6), channel_id=1, replica_groups=mesh['groups'=2,'res'=16] {'res'}, dimensions={0}, use_global_device_ids=true | all-gather | bytes 557056 | tf_op jit(solution)/shard_map/all_gather | solution.py:106
  114.9 1.6 %copy.42 = bf16[64,64,64]{1,0,2:T(8,128)(2,1)S(1)} copy(bf16[64,64,64]{2,1,0:T(8,128)(2,1)S(1)} %all_gather.11) | data formatting | bytes 1048576 | tf_op jit(solution)/shard_map/all_gather | solution.py:106
  116.5 0.1 reshape.80
  116.7 0.1 copy.43
  116.8 0.4 fusion.62
  117.3 0.1 multiply_convert_fusion.1
  117.4 0.2 fusion.48
  117.6 0.9 fusion.14
  (48 shorter events, 0.4 us)
Async XLA Ops:
  6.5 51.9 %copy-start = (bf16[1024,128]{1,0:T(8,128)(2,1)S(1)}, bf16[1024,128]{1,0:T(8,128)(2,1)}, u32[]{:S(2)}) copy-start(bf16[1024,128]{1,0:T(8,128)(2,1)} %param.22) | copy-start | bytes 786436
  6.5 3.3 %copy-start.1 = (bf16[256,4,256]{2,1,0:T(4,128)(2,1)S(1)}, bf16[256,4,256]{2,1,0:T(4,128)(2,1)}, u32[]{:S(2)}) copy-start(bf16[256,4,256]{2,1,0:T(4,128)(2,1)} %param.17) | copy-start | bytes 1572868
  6.5 4.8 %copy-start.12 = (bf16[256,32]{0,1:T(8,128)(2,1)S(1)}, bf16[256,32]{0,1:T(8,128)(2,1)}, u32[]{:S(2)}) copy-start(bf16[256,32]{0,1:T(8,128)(2,1)} %param.21) | copy-start | bytes 49156
  6.5 46.5 %copy-start.13 = (bf16[256,32]{0,1:T(8,128)(2,1)S(1)}, bf16[256,32]{0,1:T(8,128)(2,1)}, u32[]{:S(2)}) copy-start(bf16[256,32]{0,1:T(8,128)(2,1)} %param.20) | copy-start | bytes 49156
  6.5 46.5 %all-gather.2.cloned.1.call-start = ((), (), s32[]{:S(2)}) async-start(), calls=%async_computation.1 | async-start | bytes 1114112 | tf_op jit(solution)/shard_map/all_gather | solution.py:78
  55.2 3.2 %copy-start.2 = (bf16[4,64,128]{2,1,0:T(8,128)(2,1)S(1)}, bf16[4,64,128]{2,1,0:T(8,128)(2,1)}, u32[]{:S(2)}) copy-start(bf16[4,64,128]{2,1,0:T(8,128)(2,1)} %param.18) | copy-start | bytes 196612
  55.2 3.2 %copy-start.5 = (f32[128]{0:T(128)S(1)}, f32[128]{0:T(128)}, u32[]{:S(2)}) copy-start(f32[128]{0:T(128)} %param.23) | copy-start | bytes 1540
  55.3 3.9 %copy-start.8 = (bf16[128,256]{1,0:T(8,128)(2,1)S(1)}, bf16[128,256]{1,0:T(8,128)(2,1)}, u32[]{:S(2)}) copy-start(bf16[128,256]{1,0:T(8,128)(2,1)} %param.25) | copy-start | bytes 196612
  55.3 3.9 %copy-start.14 = (f32[128]{0:T(128)S(1)}, f32[128]{0:T(128)}, u32[]{:S(2)}) copy-start(f32[128]{0:T(128)} %param.24) | copy-start | bytes 1540
  59.8 24.7 %copy-start.6 = (f32[64]{0:T(128)S(1)}, f32[64]{0:T(128)}, u32[]{:S(2)}) copy-start(f32[64]{0:T(128)} %param.27) | copy-start | bytes 772
  82.0 2.6 %copy-start.3 = (bf16[64,128]{1,0:T(8,128)(2,1)S(1)}, bf16[64,128]{1,0:T(8,128)(2,1)}, u32[]{:S(2)}) copy-start(bf16[64,128]{1,0:T(8,128)(2,1)} %param.28) | copy-start | bytes 49156
  82.0 2.8 %copy-start.10 = (bf16[128,128]{1,0:T(8,128)(2,1)S(1)}, bf16[128,128]{1,0:T(8,128)(2,1)}, u32[]{:S(2)}) copy-start(bf16[128,128]{1,0:T(8,128)(2,1)} %param.26) | copy-start | bytes 98308
  82.0 3.4 %copy-start.9 = (bf16[128,256]{1,0:T(8,128)(2,1)S(1)}, bf16[128,256]{1,0:T(8,128)(2,1)}, u32[]{:S(2)}) copy-start(bf16[128,256]{1,0:T(8,128)(2,1)} %param.30) | copy-start | bytes 196612
  82.0 3.4 %copy-start.15 = (f32[128]{0:T(128)S(1)}, f32[128]{0:T(128)}, u32[]{:S(2)}) copy-start(f32[128]{0:T(128)} %param.29) | copy-start | bytes 1540
  86.6 29.9 %all-to-all-start = ((bf16[16,2,512]{2,1,0:T(2,128)(2,1)}), bf16[16,2,512]{2,1,0:T(2,128)(2,1)S(1)}, u32[]{:S(2)}, u32[]{:S(2)}) async-start(bf16[16,2,512]{2,1,0:T(2,128)(2,1)} %reshape.79), calls=%async_computation | async-start | bytes 65536 | tf_op jit(solution)/shard_map/all_to_all | solution.py:105
  114.9 2.4 %copy-start.7 = (f32[64]{0:T(128)S(1)}, f32[64]{0:T(128)}, u32[]{:S(2)}) copy-start(f32[64]{0:T(128)} %param.32) | copy-start | bytes 772
  114.9 2.6 %copy-start.4 = (bf16[64,128]{1,0:T(8,128)(2,1)S(1)}, bf16[64,128]{1,0:T(8,128)(2,1)}, u32[]{:S(2)}) copy-start(bf16[64,128]{1,0:T(8,128)(2,1)} %param.33) | copy-start | bytes 49156
  114.9 2.8 %copy-start.11 = (bf16[128,128]{1,0:T(8,128)(2,1)S(1)}, bf16[128,128]{1,0:T(8,128)(2,1)}, u32[]{:S(2)}) copy-start(bf16[128,128]{1,0:T(8,128)(2,1)} %param.31) | copy-start | bytes 98308
Sparse Core Ops, SparseCore 0:
  12.4 40.6 all-gather.1

commit v2 on v1

--- a/solution.py
+++ b/solution.py
@@ -1,6 +1,10 @@
+import functools
+
 import jax
 import jax.numpy as jnp
 from jax import lax
+from jax.experimental import pallas as pl
+from jax.experimental.pallas import tpu as pltpu
 from jax.sharding import PartitionSpec as P
 
 
@@ -110,6 +114,286 @@
     return apply_update(pair_two, in_gating, in_normed, incoming_output_weight)
 
 
+def sigmoid(values):
+    return 1.0 / (1.0 + jnp.exp(-values))
+
+
+def selection(size, source_row):
+    out_row = lax.broadcasted_iota(jnp.int32, (size, size), 0)
+    column = lax.broadcasted_iota(jnp.int32, (size, size), 1)
+    return jnp.where(source_row(out_row) == column, 1.0, 0.0).astype(jnp.bfloat16)
+
+
+def field(value, low, mask, to):
+    return ((value >> low) & mask) << to
+
+
+def dot(a, b):
+    return jnp.dot(a, b, preferred_element_type=jnp.float32)
+
+
+def packed(edges, top, bottom):
+    low = lax.broadcasted_iota(jnp.int32, top.shape, 1) < edges
+    first = jnp.where(low, top, pltpu.roll(bottom, edges, 1))
+    second = jnp.where(low, pltpu.roll(top, edges, 1), bottom)
+    return first.astype(jnp.bfloat16), second.astype(jnp.bfloat16)
+
+
+def project_block(pair, gain, weight_in, weight_gate):
+    h = weight_in.shape[1] // 4
+    w = weight_in[...]
+    normed = layer_normalize(pair, gain[...]).astype(jnp.bfloat16)
+    values = dot(normed, jnp.concatenate([w[:, :h], w[:, 2 * h : 3 * h]], axis=1))
+    gates = dot(normed, jnp.concatenate([w[:, h : 2 * h], w[:, 3 * h :]], axis=1))
+    return sigmoid(gates) * values, sigmoid(dot(normed, weight_gate[...]))
+
+
+def finish_block(pair, gating, mixed, gain, weight_out):
+    h = gain.shape[1]
+    mixed = mixed.reshape(pair.shape)
+    mixed = (mixed + pltpu.roll(mixed, h, 1))[:, :h]
+    normed = layer_normalize(mixed, gain[...]).astype(jnp.bfloat16)
+    update = dot(normed, weight_out[...])
+    return (pair + gating * update).astype(jnp.bfloat16)
+
+
+def kernel(
+    samples,
+    left_ref, right_ref, pair_ref, outer_w, outer_b,
+    gain1, edge1, gate1, mid1, out1,
+    gain2, edge2, gate2, mid2, out2,
+    o_ref,
+    lbuf, rbuf, psend, pbuf, y_scr,
+    abuf, bsend, bbuf, a_scr, b_scr, mixed_scr,
+    a2send, a2buf, b2buf, fsend, fbuf,
+    send4, recv4, send16, recv16,
+):
+    me = lax.axis_index("res")
+    z, m = me // 4, me % 4
+    barrier = pltpu.get_barrier_semaphore()
+    for d in range(1, 16):
+        pl.semaphore_signal(
+            barrier, inc=1, device_id={"res": (me + d) % 16}, device_id_type=pl.DeviceIdType.MESH
+        )
+
+    started = []
+
+    def send(src, dst, ssem, rsem, target):
+        copy = pltpu.make_async_remote_copy(
+            src_ref=src, dst_ref=dst, send_sem=ssem, recv_sem=rsem,
+            device_id={"res": target}, device_id_type=pl.DeviceIdType.MESH,
+        )
+        copy.start()
+        started.append(copy)
+        return copy
+
+    def same_z(d):
+        return z * 4 + (m + d) % 4
+
+    def same_m(d):
+        return ((z + d) % 4) * 4 + m
+
+    to_blocks = selection(
+        256, lambda r: field(r, 6, 3, 2) + field(r, 4, 3, 4) + field(r, 2, 3, 0) + field(r, 0, 3, 6)
+    )
+    psend[...] = dot(to_blocks, pair_ref[...]).astype(jnp.bfloat16).reshape(4, 64, 128)
+    lbuf[m] = left_ref[...]
+    rbuf[z] = right_ref[...]
+    pbuf[m] = psend[m]
+
+    pl.semaphore_wait(barrier, 15)
+    r_copies = [
+        send(right_ref, rbuf.at[z], send4.at[0, d], recv4.at[0, d], same_m(d)) for d in range(1, 4)
+    ]
+    l_copies = [
+        send(left_ref, lbuf.at[m], send4.at[1, d], recv4.at[1, d], same_z(d)) for d in range(1, 4)
+    ]
+    p_copies = [
+        send(psend.at[(m + d) % 4], pbuf.at[m], send4.at[2, d], recv4.at[2, d], same_z(d))
+        for d in range(1, 4)
+    ]
+    order_left = selection(
+        512, lambda r: field(r, 2, 3, 7) + field(r, 0, 3, 5) + field(r, 4, 7, 2) + field(r, 7, 3, 0)
+    )
+    for copy in l_copies:
+        copy.wait_recv()
+    left_t = sum(
+        lax.dot_general(
+            order_left[:, k * 128 : (k + 1) * 128], lbuf[k], (((1,), (1,)), ((), ())),
+            preferred_element_type=jnp.float32,
+        )
+        for k in range(4)
+    ).astype(jnp.bfloat16)
+    for copy in p_copies:
+        copy.wait_recv()
+    order_pair = selection(
+        256, lambda r: field(r, 2, 3, 6) + field(r, 6, 3, 4) + field(r, 4, 3, 2) + field(r, 0, 3, 0)
+    )
+    state = dot(order_pair, pbuf[...].reshape(256, 128))
+
+    for copy in r_copies:
+        copy.wait_recv()
+    lane = lax.broadcasted_iota(jnp.int32, (128, 128), 1)
+    for b in range(4):
+        outer = dot(left_t, rbuf[b])
+        x = [outer[k * 128 : (k + 1) * 128] for k in range(4)]
+        low = lane < 64
+        for u, v in ((0, 2), (1, 3)):
+            x[u], x[v] = (
+                jnp.where(low, x[u], pltpu.roll(x[v], 64, 1)),
+                jnp.where(low, pltpu.roll(x[u], 64, 1), x[v]),
+            )
+        low = (lane & 32) == 0
+        for u, v in ((0, 1), (2, 3)):
+            x[u], x[v] = (
+                jnp.where(low, x[u], pltpu.roll(x[v], 32, 1)),
+                jnp.where(low, pltpu.roll(x[u], 96, 1), x[v]),
+            )
+        for k in range(4):
+            y_scr[:, b * 4 + k] = (x[k] * (1.0 / samples)).astype(jnp.bfloat16).reshape(8, 16, 128)
+    update = sum(
+        dot(y_scr[a].reshape(256, 128), outer_w[a * 128 : (a + 1) * 128, :]) for a in range(8)
+    )
+    pair = (state + (update + outer_b[...])).astype(jnp.bfloat16).astype(jnp.float32)
+
+    edges, gating = project_block(pair, gain1, edge1, gate1)
+    a_half, b_half = packed(64, edges[:128], edges[128:])
+    to_rows = selection(128, lambda r: field(r, 2, 7, 4) + field(r, 5, 3, 2) + field(r, 0, 3, 0))
+    bsend[...] = dot(to_rows, b_half).astype(jnp.bfloat16).reshape(4, 32, 128)
+    abuf[m] = a_half
+    bbuf[z, m] = bsend[m]
+    b_copies = [
+        send(bsend.at[(me + d) % 4], bbuf.at[z, m], send16.at[0, d], recv16.at[0, d], (me + d) % 16)
+        for d in range(1, 16)
+    ]
+    a_copies = [
+        send(abuf.at[m], abuf.at[m], send4.at[3, d], recv4.at[3, d], same_z(d)) for d in range(1, 4)
+    ]
+    for copy in a_copies + b_copies:
+        copy.wait_recv()
+    a_scr[...] = abuf[...].astype(jnp.float32).reshape(32, 16, 128)
+    b_scr[...] = bbuf[...].astype(jnp.float32)
+
+    def outgoing(j, carry):
+        zj, rj = j // 4, j % 4
+        total = jnp.zeros((16, 128), jnp.float32)
+        for k in range(32):
+            total += a_scr[k] * b_scr[zj, k // 8, pl.ds((k % 8) * 4 + rj, 1), :]
+        mixed_scr[j] = total
+        return carry
+
+    lax.fori_loop(0, 16, outgoing, 0)
+    pair = finish_block(pair, gating, mixed_scr[...], mid1, out1).astype(jnp.float32)
+
+    edges, gating = project_block(pair, gain2, edge2, gate2)
+    halves = edges.reshape(16, 2, 8, 128)
+    a_half, b_half = packed(64, halves[:, 0].reshape(128, 128), halves[:, 1].reshape(128, 128))
+    a2send[...] = a_half.reshape(4, 32, 128)
+    b2buf[z] = b_half
+    a2buf[z, m] = a2send[z]
+    b2_copies = [
+        send(b2buf.at[z], b2buf.at[z], send4.at[4, d], recv4.at[4, d], same_m(d)) for d in range(1, 4)
+    ]
+    a2_copies = [
+        send(
+            a2send.at[((me + d) % 16) // 4], a2buf.at[z, m], send16.at[1, d], recv16.at[1, d],
+            (me + d) % 16,
+        )
+        for d in range(1, 16)
+    ]
+    by_step = selection(128, lambda r: field(r, 2, 3, 5) + field(r, 0, 3, 3) + field(r, 4, 7, 0))
+    for copy in a2_copies:
+        copy.wait_recv()
+    for k in range(4):
+        a_scr[k * 8 : (k + 1) * 8] = dot(by_step, a2buf[k].reshape(128, 128)).reshape(8, 16, 128)
+    for copy in b2_copies:
+        copy.wait_recv()
+    b_scr[...] = b2buf[...].astype(jnp.float32).reshape(b_scr.shape)
+
+    def incoming(j, carry):
+        jb, jr = j // 4, j % 4
+        total = jnp.zeros((16, 128), jnp.float32)
+        for k in range(32):
+            total += a_scr[k] * b_scr[k // 8, jb, pl.ds(jr * 8 + k % 8, 1), :]
+        mixed_scr[j] = total
+        return carry
+
+    lax.fori_loop(0, 16, incoming, 0)
+    done = finish_block(pair, gating, mixed_scr[...], mid2, out2)
+
+    from_blocks = selection(
+        256, lambda r: field(r, 2, 3, 6) + field(r, 0, 3, 4) + field(r, 6, 3, 2) + field(r, 4, 3, 0)
+    )
+    fsend[...] = dot(from_blocks, done).astype(jnp.bfloat16).reshape(4, 64, 128)
+    fbuf[m] = fsend[m]
+    f_copies = [
+        send(fsend.at[(m + d) % 4], fbuf.at[m], send4.at[5, d], recv4.at[5, d], same_z(d))
+        for d in range(1, 4)
+    ]
+    for copy in f_copies:
+        copy.wait_recv()
+    o_ref[...] = fbuf[...]
+    for copy in started:
+        copy.wait_send()
+
+
+def blocks(*args):
+    embedding, pair_state, norm_scale, former, latter = args[:5]
+    samples, rows, channels = embedding.shape
+    normed = layer_normalize(embedding.astype(jnp.float32), norm_scale).astype(jnp.bfloat16)
+    left, right = (
+        jnp.einsum("vfd,dl->vfl", normed, w, preferred_element_type=jnp.float32)
+        .astype(jnp.bfloat16)
+        .reshape(samples, -1)
+        for w in (former, latter)
+    )
+    rest = [a.reshape(1, -1) if a.ndim == 1 else a for a in args[5:]]
+    bf16, f32 = jnp.bfloat16, jnp.float32
+    vmem = pl.BlockSpec(memory_space=pltpu.VMEM)
+    out = pl.pallas_call(
+        functools.partial(kernel, samples),
+        out_shape=jax.ShapeDtypeStruct((4, 64, 128), bf16),
+        in_specs=[vmem] * (3 + len(rest)),
+        out_specs=vmem,
+        scratch_shapes=[
+            pltpu.VMEM((4, 256, 128), bf16),
+            pltpu.VMEM((4, 256, 128), bf16),
+            pltpu.VMEM((4, 64, 128), bf16),
+            pltpu.VMEM((4, 64, 128), bf16),
+            pltpu.VMEM((8, 16, 16, 128), bf16),
+            pltpu.VMEM((4, 128, 128), bf16),
+            pltpu.VMEM((4, 32, 128), bf16),
+            pltpu.VMEM((4, 4, 32, 128), bf16),
+            pltpu.VMEM((32, 16, 128), f32),
+            pltpu.VMEM((4, 4, 32, 128), f32),
+            pltpu.VMEM((16, 16, 128), f32),
+            pltpu.VMEM((4, 32, 128), bf16),
+            pltpu.VMEM((4, 4, 32, 128), bf16),
+            pltpu.VMEM((4, 128, 128), bf16),
+            pltpu.VMEM((4, 64, 128), bf16),
+            pltpu.VMEM((4, 64, 128), bf16),
+            pltpu.SemaphoreType.DMA((6, 4)),
+            pltpu.SemaphoreType.DMA((6, 4)),
+            pltpu.SemaphoreType.DMA((2, 16)),
+            pltpu.SemaphoreType.DMA((2, 16)),
+        ],
+        compiler_params=pltpu.CompilerParams(
+            collective_id=0, has_side_effects=True, vmem_limit_bytes=32 * 1024 * 1024
+        ),
+    )(left, right, pair_state.reshape(256, 128), *rest)
+    return out.reshape(4, 4, 4, 4, 128).transpose(1, 2, 0, 3, 4).reshape(pair_state.shape)
+
+
+def fits_blocks(mesh, embedding, pair_state, former, edge_weight):
+    return (
+        mesh.shape["res"] == 16
+        and pair_state.shape[1:] == (64, 128)
+        and embedding.shape[0] // mesh.shape["groups"] == 256
+        and former.shape[1] == 32
+        and edge_weight.shape == (128, 256)
+    )
+
+
 def solution(mesh):
     in_specs = (
         P("groups", "res", None),
@@ -131,4 +415,12 @@
         P(),
     )
     out_specs = P(("groups", "res"), None, None)
-    return jax.shard_map(shards, mesh=mesh, in_specs=in_specs, out_specs=out_specs, check_vma=False)
+
+    def program(*args):
+        blocked = fits_blocks(mesh, args[0], args[1], args[3], args[8])
+        return jax.shard_map(
+            blocks if blocked else shards,
+            mesh=mesh, in_specs=in_specs, out_specs=out_specs, check_vma=False,
+        )(*args)
+
+    return program

time: 126 us -> 40.7 us (0.32)
  blocking collectives: 47 us -> 0 us
  waiting for transfers between devices: 40.8 us -> 0 us
  Pallas kernels: 0 us -> 34 us
  between operations: 13.7 us -> 0.18 us
  matrix products: 6.81 us -> 0.48 us
  local copies, waits for them, and re-layouts: 7.64 us -> 2.74 us
  starting transfers between devices: 3.53 us -> 0 us
  other arithmetic: 5.86 us -> 3.05 us
    all_gather x2 -> x0, blocking collectives: 47 us -> none  [the longest x1 24.7 us: shards(): lax.all_gather(in_right, 'res', axis=0, tiled=True)]
    all_gather x1 -> x0, waiting for transfers between devices: 40.8 us -> none  [shards(): lax.all_gather(right_factor, 'res', axis=1, tiled=True)]
    pallas_call x0 -> x1, Pallas kernels: none -> 34 us  [blocks(): pl.pallas_call(functools.partial(kernel, samples), out_shape=jax.ShapeDty...]
    dot_general x11 -> x2, matrix products: 6.81 us -> 0.48 us  [blocks(): jnp.einsum('vfd,dl->vfl', normed, w, preferred_element_type=jnp.float32)]
    all_to_all x1 -> x0, starting transfers between devices: 3.5 us -> none  [shards(): lax.all_to_all(in_left, 'res', split_axis=1, concat_axis=0, tiled=True)]
    convert_element_type x3 -> x0, local copies, waits for them, and re-layouts: 3.31 us -> none  [the longest x1 3.14 us: shards(): outer.reshape(outer.shape[0], outer.shape[1], -1).astype(jnp.bfloat16)]
    all_gather x2 -> x0, local copies, waits for them, and re-layouts: 3.29 us -> none  [the longest x1 1.65 us: shards(): lax.all_gather(edge_right, 'res', axis=0, tiled=True)]
    reduce_sum x5 -> x1, other arithmetic: 2.3 us -> 0.84 us  [layer_normalize(): variance = jnp.mean(centred * centred, axis=-1, keepdims=True)]
  transfers between devices with their start and end apart: 2 -> 0, of which waited for: 1 -> 0; matrix products, arithmetic and copies ran while one was open for 1% -> 0% of each run, Pallas kernels for 0% -> 0%
where the time goes in v2:
time: 40.7 us; the launch traced here: 40.4 us
  Pallas kernels  34 us (84%)
  other arithmetic  3.05 us (7%)
  local copies, waits for them, and re-layouts  2.74 us (7%)
  matrix products  0.48 us (1%)
    pallas_call x1, Pallas kernels, blocks(): pl.pallas_call(functools.partial(kernel, samples), out_shape=jax.ShapeDty...  34 us
    unnamed x34, local copies, waits for them, and re-layouts  1.84 us
    reduce_sum x1, other arithmetic, layer_normalize(): mean_val = jnp.mean(values, axis=-1, keepdims=True)  1.46 us
    reduce_sum x1, other arithmetic, layer_normalize(): variance = jnp.mean(centred * centred, axis=-1, keepdims=True)  0.84 us

profile of v2, /device:TPU:0, one launch (start us, length us, event | category | flops | bytes accessed | tf_op | source)
XLA Modules:
  0.0 40.4 jit_solution(13352942323705740968)
XLA Ops:
  0.0 0.0 copy-start
  0.0 1.5 %convert_reduce_fusion = f32[256,4]{1,0:T(8,128)S(1)} fusion(bf16[256,4,256]{2,1,0:T(4,128)(2,1)} %param.17), kind=kLoop, calls=%fused_computation.1 | loop fusion | flops 523264 | bytes 528384 | tf_op jit(solution)/shard_map/reduce_sum | solution.py:12
  1.5 0.0 copy-done.14
  1.5 0.8 %fusion.4 = f32[256,4]{1,0:T(8,128)S(1)} fusion(bf16[256,4,256]{2,1,0:T(4,128)(2,1)S(1)} %copy-done.14, f32[256,4]{1,0:T(8,128)S(1)} %broadcast_multiply_fusion), kind=kLoop, calls=%fused_computation.8 | loop fusion | flops 1047552 | bytes 532480 | tf_op jit(solution)/shard_map/reduce_sum | solution.py:14
  2.3 0.0 copy-start.15
  2.4 0.6 %copy-done.15 = f32[256]{0:T(256)S(1)} copy-done((f32[256]{0:T(256)S(1)}, f32[256]{0:T(256)}, u32[]{:S(2)}) %copy-start.15) | copy-done | bytes 1048
  3.0 0.7 %fusion.3 = bf16[256,4,256]{2,1,0:T(4,128)(2,1)S(1)} fusion(bf16[256,4,256]{2,1,0:T(4,128)(2,1)S(1)} %copy-done.14, f32[256]{0:T(256)S(1)} %copy-done.15, f32[256,4]{1,0:T(8,128)S(1)} %add_sqrt_fusion, f32[256,4]{1,0:T(8,128)S(1)} %broadcast_multiply_fusion), kind=kLoop, calls=%fused_computation.7 | loop fusion | flops 1310720 | bytes 1057792 | tf_op jit(solution)/shard_map/convert_element_type | solution.py:343
  3.7 0.0 copy-done
  3.7 0.0 copy-start.16
  3.8 0.2 convolution_convert_fusion
  4.0 0.5 %copy-done.16 = bf16[256,32]{0,1:T(8,128)(2,1)S(1)} copy-done((bf16[256,32]{0,1:T(8,128)(2,1)S(1)}, bf16[256,32]{0,1:T(8,128)(2,1)}, u32[]{:S(2)}) %copy-start.16) | copy-done | bytes 16408
  4.5 0.0 copy-start.6
  4.5 0.0 copy-start.7
  4.5 0.0 copy-start.8
  4.5 0.2 convolution_convert_fusion.1
  4.8 0.1 copy.25.left_ref
  4.9 0.0 copy-start.9
  4.9 0.0 copy-start.10
  4.9 0.0 copy-start.11
  4.9 0.0 copy-start.12
  5.0 0.0 copy-start.13
  5.0 0.1 copy.26.right_ref
  5.1 0.2 copy-done.2
  5.3 0.0 copy-done.3
  5.3 0.0 copy-done.4
  5.4 0.0 copy-done.5
  5.4 0.0 copy-done.6
  5.4 0.0 copy-done.7
  5.4 0.4 copy-done.1
  5.8 0.0 copy-done.11
  5.8 34.0 %shard_map.163 = bf16[4,64,128]{2,1,0:T(8,128)(2,1)S(1)} custom-call(bf16[256,128]{1,0:T(8,128)(2,1)S(1)} %copy.25.left_ref, bf16[256,128]{1,0:T(8,128)(2,1)S(1)} %copy.26.right_ref, bf16[256,128]{1,0:T(8,128)(2,1)S(1)} %bitcast.19, bf16[1024,128]{1,0:T(8,128)(2,1)S(1)} %copy-done.1, f32[1,128]{1,0:T(1,128)S(1)} %bitcast.20, f32[1,128]{1,0:T(1,128)S(1)} %bitcast.21, ...), custom_call_target="tpu_custom_call" | custom-call | tf_op jit(solution)/shard_map/pallas_call | solution.py:353
  39.8 0.7 %copy.27 = bf16[4,4,4,4,128]{4,3,2,1,0:T(4,128)(2,1)} copy(bf16[4,4,4,4,128]{4,3,1,0,2:T(4,128)(2,1)S(1)} %bitcast.18) | data formatting | bytes 131072 | tf_op jit(solution)/shard_map/transpose | solution.py:384
  (13 shorter events, 0.1 us)
Async XLA Ops:
  0.0 3.7 %copy-start = (bf16[256,32]{0,1:T(8,128)(2,1)S(1)}, bf16[256,32]{0,1:T(8,128)(2,1)}, u32[]{:S(2)}) copy-start(bf16[256,32]{0,1:T(8,128)(2,1)} %param.21) | copy-start | bytes 49156
  0.0 1.5 %copy-start.14 = (bf16[256,4,256]{2,1,0:T(4,128)(2,1)S(1)}, bf16[256,4,256]{2,1,0:T(4,128)(2,1)}, u32[]{:S(2)}) copy-start(bf16[256,4,256]{2,1,0:T(4,128)(2,1)} %param.17) | copy-start | bytes 1572868
  2.3 0.7 %copy-start.15 = (f32[256]{0:T(256)S(1)}, f32[256]{0:T(256)}, u32[]{:S(2)}) copy-start(f32[256]{0:T(256)} %param.19) | copy-start | bytes 3076
  3.7 0.7 %copy-start.16 = (bf16[256,32]{0,1:T(8,128)(2,1)S(1)}, bf16[256,32]{0,1:T(8,128)(2,1)}, u32[]{:S(2)}) copy-start(bf16[256,32]{0,1:T(8,128)(2,1)} %param.20) | copy-start | bytes 49156
  4.5 0.8 %copy-start.2 = (bf16[4,64,128]{2,1,0:T(8,128)(2,1)S(1)}, bf16[4,64,128]{2,1,0:T(8,128)(2,1)}, u32[]{:S(2)}) copy-start(bf16[4,64,128]{2,1,0:T(8,128)(2,1)} %param.18) | copy-start | bytes 196612
  4.5 0.9 %copy-start.3 = (bf16[128,256]{1,0:T(8,128)(2,1)S(1)}, bf16[128,256]{1,0:T(8,128)(2,1)}, u32[]{:S(2)}) copy-start(bf16[128,256]{1,0:T(8,128)(2,1)} %edge1.1) | copy-start | bytes 196612
  4.5 0.9 %copy-start.4 = (bf16[128,256]{1,0:T(8,128)(2,1)S(1)}, bf16[128,256]{1,0:T(8,128)(2,1)}, u32[]{:S(2)}) copy-start(bf16[128,256]{1,0:T(8,128)(2,1)} %edge2.1) | copy-start | bytes 196612
  4.5 0.9 %copy-start.5 = (bf16[128,128]{1,0:T(8,128)(2,1)S(1)}, bf16[128,128]{1,0:T(8,128)(2,1)}, u32[]{:S(2)}) copy-start(bf16[128,128]{1,0:T(8,128)(2,1)} %gate1.1) | copy-start | bytes 98308
  4.5 0.9 %copy-start.6 = (bf16[128,128]{1,0:T(8,128)(2,1)S(1)}, bf16[128,128]{1,0:T(8,128)(2,1)}, u32[]{:S(2)}) copy-start(bf16[128,128]{1,0:T(8,128)(2,1)} %gate2.1) | copy-start | bytes 98308
  4.5 0.9 %copy-start.7 = (bf16[64,128]{1,0:T(8,128)(2,1)S(1)}, bf16[64,128]{1,0:T(8,128)(2,1)}, u32[]{:S(2)}) copy-start(bf16[64,128]{1,0:T(8,128)(2,1)} %out1.1) | copy-start | bytes 49156
  4.5 0.9 %copy-start.8 = (bf16[64,128]{1,0:T(8,128)(2,1)S(1)}, bf16[64,128]{1,0:T(8,128)(2,1)}, u32[]{:S(2)}) copy-start(bf16[64,128]{1,0:T(8,128)(2,1)} %out2.1) | copy-start | bytes 49156
  4.8 1.0 %copy-start.1 = (bf16[1024,128]{1,0:T(8,128)(2,1)S(1)}, bf16[1024,128]{1,0:T(8,128)(2,1)}, u32[]{:S(2)}) copy-start(bf16[1024,128]{1,0:T(8,128)(2,1)} %outer_w.1) | copy-start | bytes 786436
  4.9 0.9 %copy-start.9 = (f32[128]{0:T(128)S(1)}, f32[128]{0:T(128)}, u32[]{:S(2)}) copy-start(f32[128]{0:T(128)} %param.23) | copy-start | bytes 1540
  4.9 0.9 %copy-start.10 = (f32[128]{0:T(128)S(1)}, f32[128]{0:T(128)}, u32[]{:S(2)}) copy-start(f32[128]{0:T(128)} %param.24) | copy-start | bytes 1540
  4.9 0.8 %copy-start.11 = (f32[64]{0:T(128)S(1)}, f32[64]{0:T(128)}, u32[]{:S(2)}) copy-start(f32[64]{0:T(128)} %param.27) | copy-start | bytes 772
  4.9 0.8 %copy-start.12 = (f32[128]{0:T(128)S(1)}, f32[128]{0:T(128)}, u32[]{:S(2)}) copy-start(f32[128]{0:T(128)} %param.29) | copy-start | bytes 1540
  5.0 0.8 %copy-start.13 = (f32[64]{0:T(128)S(1)}, f32[64]{0:T(128)}, u32[]{:S(2)}) copy-start(f32[64]{0:T(128)} %param.32) | copy-start | bytes 772

commit v3 on v2

--- a/solution.py
+++ b/solution.py
@@ -159,11 +159,11 @@
 
 def kernel(
     samples,
-    left_ref, right_ref, pair_ref, outer_w, outer_b,
+    msa_ref, msa_gain, former, latter, pair_ref, outer_w, outer_b,
     gain1, edge1, gate1, mid1, out1,
     gain2, edge2, gate2, mid2, out2,
     o_ref,
-    lbuf, rbuf, psend, pbuf, y_scr,
+    msa_scr, lbuf, rbuf, psend, pbuf, y_scr,
     abuf, bsend, bbuf, a_scr, b_scr, mixed_scr,
     a2send, a2buf, b2buf, fsend, fbuf,
     send4, recv4, send16, recv16,
@@ -197,16 +197,25 @@
         256, lambda r: field(r, 6, 3, 2) + field(r, 4, 3, 4) + field(r, 2, 3, 0) + field(r, 0, 3, 6)
     )
     psend[...] = dot(to_blocks, pair_ref[...]).astype(jnp.bfloat16).reshape(4, 64, 128)
-    lbuf[m] = left_ref[...]
-    rbuf[z] = right_ref[...]
     pbuf[m] = psend[m]
 
+    msa_scr[...] = msa_ref[...].astype(jnp.float32)
+    weights = jnp.concatenate([former[...]] * 4 + [latter[...]] * 4, axis=1)
+    position = (lax.broadcasted_iota(jnp.int32, weights.shape, 1) >> 5) & 3
+    factors = jnp.zeros((msa_ref.shape[0], 256), jnp.float32)
+    for r in range(4):
+        normed = layer_normalize(msa_scr[:, r, :], msa_gain[...]).astype(jnp.bfloat16)
+        own = jnp.where(position == r, weights.astype(jnp.float32), 0.0).astype(jnp.bfloat16)
+        factors += dot(normed, own)
+    lbuf[m] = factors[:, :128].astype(jnp.bfloat16)
+    rbuf[z] = factors[:, 128:].astype(jnp.bfloat16)
+
     pl.semaphore_wait(barrier, 15)
-    r_copies = [
-        send(right_ref, rbuf.at[z], send4.at[0, d], recv4.at[0, d], same_m(d)) for d in range(1, 4)
+    _ = [
+        send(rbuf.at[z], rbuf.at[z], send4.at[0, d], recv4.at[0, z], same_m(d)) for d in range(1, 4)
     ]
     l_copies = [
-        send(left_ref, lbuf.at[m], send4.at[1, d], recv4.at[1, d], same_z(d)) for d in range(1, 4)
+        send(lbuf.at[m], lbuf.at[m], send4.at[1, d], recv4.at[1, d], same_z(d)) for d in range(1, 4)
     ]
     p_copies = [
         send(psend.at[(m + d) % 4], pbuf.at[m], send4.at[2, d], recv4.at[2, d], same_z(d))
@@ -231,10 +240,16 @@
     )
     state = dot(order_pair, pbuf[...].reshape(256, 128))
 
-    for copy in r_copies:
-        copy.wait_recv()
+    near = jnp.where(z == 0, 1, z - 1)
+    middle = jnp.where(z == 0, 2, jnp.where(z == 3, 1, z + 1))
     lane = lax.broadcasted_iota(jnp.int32, (128, 128), 1)
-    for b in range(4):
+    for b in (z, near, middle, 6 - z - near - middle):
+        if b is not z:
+            pltpu.make_async_remote_copy(
+                src_ref=rbuf.at[z], dst_ref=rbuf.at[b], send_sem=send4.at[0, 0],
+                recv_sem=recv4.at[0, b], device_id={"res": b * 4 + m},
+                device_id_type=pl.DeviceIdType.MESH,
+            ).wait_recv()
         outer = dot(left_t, rbuf[b])
         x = [outer[k * 128 : (k + 1) * 128] for k in range(4)]
         low = lane < 64
@@ -282,7 +297,7 @@
         mixed_scr[j] = total
         return carry
 
-    lax.fori_loop(0, 16, outgoing, 0)
+    lax.fori_loop(0, 16, outgoing, 0, unroll=4)
     pair = finish_block(pair, gating, mixed_scr[...], mid1, out1).astype(jnp.float32)
 
     edges, gating = project_block(pair, gain2, edge2, gate2)
@@ -291,15 +306,15 @@
     a2send[...] = a_half.reshape(4, 32, 128)
     b2buf[z] = b_half
     a2buf[z, m] = a2send[z]
-    b2_copies = [
-        send(b2buf.at[z], b2buf.at[z], send4.at[4, d], recv4.at[4, d], same_m(d)) for d in range(1, 4)
-    ]
     a2_copies = [
         send(
             a2send.at[((me + d) % 16) // 4], a2buf.at[z, m], send16.at[1, d], recv16.at[1, d],
             (me + d) % 16,
         )
         for d in range(1, 16)
+    ]
+    b2_copies = [
+        send(b2buf.at[z], b2buf.at[z], send4.at[4, d], recv4.at[4, d], same_m(d)) for d in range(1, 4)
     ]
     by_step = selection(128, lambda r: field(r, 2, 3, 5) + field(r, 0, 3, 3) + field(r, 4, 7, 0))
     for copy in a2_copies:
@@ -318,7 +333,7 @@
         mixed_scr[j] = total
         return carry
 
-    lax.fori_loop(0, 16, incoming, 0)
+    lax.fori_loop(0, 16, incoming, 0, unroll=4)
     done = finish_block(pair, gating, mixed_scr[...], mid2, out2)
 
     from_blocks = selection(
@@ -339,23 +354,17 @@
 
 def blocks(*args):
     embedding, pair_state, norm_scale, former, latter = args[:5]
-    samples, rows, channels = embedding.shape
-    normed = layer_normalize(embedding.astype(jnp.float32), norm_scale).astype(jnp.bfloat16)
-    left, right = (
-        jnp.einsum("vfd,dl->vfl", normed, w, preferred_element_type=jnp.float32)
-        .astype(jnp.bfloat16)
-        .reshape(samples, -1)
-        for w in (former, latter)
-    )
+    samples = embedding.shape[0]
     rest = [a.reshape(1, -1) if a.ndim == 1 else a for a in args[5:]]
     bf16, f32 = jnp.bfloat16, jnp.float32
     vmem = pl.BlockSpec(memory_space=pltpu.VMEM)
     out = pl.pallas_call(
         functools.partial(kernel, samples),
         out_shape=jax.ShapeDtypeStruct((4, 64, 128), bf16),
-        in_specs=[vmem] * (3 + len(rest)),
+        in_specs=[vmem] * (5 + len(rest)),
         out_specs=vmem,
         scratch_shapes=[
+            pltpu.VMEM(embedding.shape, f32),
             pltpu.VMEM((4, 256, 128), bf16),
             pltpu.VMEM((4, 256, 128), bf16),
             pltpu.VMEM((4, 64, 128), bf16),
@@ -380,7 +389,7 @@
         compiler_params=pltpu.CompilerParams(
             collective_id=0, has_side_effects=True, vmem_limit_bytes=32 * 1024 * 1024
         ),
-    )(left, right, pair_state.reshape(256, 128), *rest)
+    )(embedding, norm_scale.reshape(1, -1), former, latter, pair_state.reshape(256, 128), *rest)
     return out.reshape(4, 4, 4, 4, 128).transpose(1, 2, 0, 3, 4).reshape(pair_state.shape)
 
 

time: 40.7 us -> 41.4 us (1.017)
  local copies, waits for them, and re-layouts: 2.74 us -> 7.48 us
  other arithmetic: 3.05 us -> 0 us
  Pallas kernels: 34 us -> 33.2 us
  matrix products: 0.48 us -> 0 us
    unnamed x34 -> x32, local copies, waits for them, and re-layouts: 1.84 us -> 6.83 us
    reduce_sum x2 -> x0, other arithmetic: 2.3 us -> none  [the longest x1 1.46 us: layer_normalize(): mean_val = jnp.mean(values, axis=-1, keepdims=True)]
    pallas_call x1, Pallas kernels: 34 us -> 33.2 us  [blocks(): pl.pallas_call(functools.partial(kernel, samples), out_shape=jax.ShapeDty...]
    convert_element_type x1 -> x0, other arithmetic: 0.7 us -> none  [blocks(): layer_normalize(embedding.astype(jnp.float32), norm_scale)]
    dot_general x2 -> x0, matrix products: 0.48 us -> none  [blocks(): jnp.einsum('vfd,dl->vfl', normed, w, preferred_element_type=jnp.float32)]
where the time goes in v3:
time: 41.4 us; the launch traced here: 40.8 us
  Pallas kernels  33.2 us (80%)
  local copies, waits for them, and re-layouts  7.48 us (18%)
    pallas_call x1, Pallas kernels, blocks(): pl.pallas_call(functools.partial(kernel, samples), out_shape=jax.ShapeDty...  33.2 us
    unnamed x32, local copies, waits for them, and re-layouts  6.83 us

profile of v3, /device:TPU:0, one launch (start us, length us, event | category | flops | bytes accessed | tf_op | source)
XLA Modules:
  0.0 40.8 jit_solution(4775231081979515711)
XLA Ops:
  0.0 0.0 copy-start.11
  0.0 0.0 copy-start.12
  0.0 0.0 copy-start.13
  0.0 0.0 copy-start.14
  0.0 0.0 copy-start.9
  0.0 0.0 copy-start.10
  0.0 0.0 copy-start.2
  0.0 0.0 copy-start.3
  0.0 0.9 %copy.18.former = bf16[256,32]{1,0:T(8,128)(2,1)S(1)} copy(bf16[256,32]{0,1:T(8,128)(2,1)} %param.20) | data formatting | bytes 32768 | tf_op args[3]
  1.0 0.0 copy-start.5
  1.0 0.8 %copy.19.latter = bf16[256,32]{1,0:T(8,128)(2,1)S(1)} copy(bf16[256,32]{0,1:T(8,128)(2,1)} %param.21) | data formatting | bytes 32768 | tf_op args[4]
  1.8 0.0 copy-done.11
  1.8 0.0 copy-done.12
  1.9 0.0 copy-done.13
  1.9 0.0 copy-done.14
  1.9 0.0 copy-done.9
  1.9 0.0 copy-done.10
  1.9 0.0 copy-done.2
  1.9 0.0 copy-done.3
  1.9 0.0 copy-done.5
  1.9 0.0 copy-start
  1.9 1.0 %copy-done = bf16[256,4,256]{2,1,0:T(4,128)(2,1)S(1)} copy-done((bf16[256,4,256]{2,1,0:T(4,128)(2,1)S(1)}, bf16[256,4,256]{2,1,0:T(4,128)(2,1)}, u32[]{:S(2)}) %copy-start) | copy-done | bytes 524312
  3.0 0.0 copy-start.1
  3.0 0.9 %copy-done.1 = bf16[1024,128]{1,0:T(8,128)(2,1)S(1)} copy-done((bf16[1024,128]{1,0:T(8,128)(2,1)S(1)}, bf16[1024,128]{1,0:T(8,128)(2,1)}, u32[]{:S(2)}) %copy-start.1) | copy-done | bytes 262168
  3.9 0.0 copy-start.4
  3.9 0.8 %copy-done.4 = bf16[128,256]{1,0:T(8,128)(2,1)S(1)} copy-done((bf16[128,256]{1,0:T(8,128)(2,1)S(1)}, bf16[128,256]{1,0:T(8,128)(2,1)}, u32[]{:S(2)}) %copy-start.4) | copy-done | bytes 65560
  4.8 0.0 copy-start.6
  4.8 0.8 %copy-done.6 = bf16[128,128]{1,0:T(8,128)(2,1)S(1)} copy-done((bf16[128,128]{1,0:T(8,128)(2,1)S(1)}, bf16[128,128]{1,0:T(8,128)(2,1)}, u32[]{:S(2)}) %copy-start.6) | copy-done | bytes 32792
  5.5 0.7 %copy-done.7 = bf16[64,128]{1,0:T(8,128)(2,1)S(1)} copy-done((bf16[64,128]{1,0:T(8,128)(2,1)S(1)}, bf16[64,128]{1,0:T(8,128)(2,1)}, u32[]{:S(2)}) %copy-start.7) | copy-done | bytes 16408
  6.2 0.7 %copy-done.8 = bf16[64,128]{1,0:T(8,128)(2,1)S(1)} copy-done((bf16[64,128]{1,0:T(8,128)(2,1)S(1)}, bf16[64,128]{1,0:T(8,128)(2,1)}, u32[]{:S(2)}) %copy-start.8) | copy-done | bytes 16408
  7.0 33.2 %shard_map.163 = bf16[4,64,128]{2,1,0:T(8,128)(2,1)S(1)} custom-call(bf16[256,4,256]{2,1,0:T(4,128)(2,1)S(1)} %copy-done, f32[1,256]{1,0:T(1,128)S(1)} %bitcast.13, bf16[256,32]{1,0:T(8,128)(2,1)S(1)} %copy.18.former, bf16[256,32]{1,0:T(8,128)(2,1)S(1)} %copy.19.latter, bf16[256,128]{1,0:T(8,128)(2,1)S(1)} %bitcast.12, bf16[1024,128]{1,0:T(8,128)(2,1)S(1)} %copy-done.1, ...), custom_call_target="tpu_custom_call" | custom-call | tf_op jit(solution)/shard_map/pallas_call | solution.py:361
  40.2 0.7 %copy.20 = bf16[4,4,4,4,128]{4,3,2,1,0:T(4,128)(2,1)} copy(bf16[4,4,4,4,128]{4,3,1,0,2:T(4,128)(2,1)S(1)} %bitcast.11) | data formatting | bytes 131072 | tf_op jit(solution)/shard_map/transpose | solution.py:393
  (2 shorter events, 0.0 us)
Async XLA Ops:
  0.0 1.8 %copy-start.11 = (f32[128]{0:T(128)S(1)}, f32[128]{0:T(128)}, u32[]{:S(2)}) copy-start(f32[128]{0:T(128)} %param.24) | copy-start | bytes 1540
  0.0 1.8 %copy-start.12 = (f32[64]{0:T(128)S(1)}, f32[64]{0:T(128)}, u32[]{:S(2)}) copy-start(f32[64]{0:T(128)} %param.27) | copy-start | bytes 772
  0.0 1.8 %copy-start.13 = (f32[128]{0:T(128)S(1)}, f32[128]{0:T(128)}, u32[]{:S(2)}) copy-start(f32[128]{0:T(128)} %param.29) | copy-start | bytes 1540
  0.0 1.9 %copy-start.14 = (f32[64]{0:T(128)S(1)}, f32[64]{0:T(128)}, u32[]{:S(2)}) copy-start(f32[64]{0:T(128)} %param.32) | copy-start | bytes 772
  0.0 1.9 %copy-start.9 = (f32[256]{0:T(256)S(1)}, f32[256]{0:T(256)}, u32[]{:S(2)}) copy-start(f32[256]{0:T(256)} %param.19) | copy-start | bytes 3076
  0.0 1.9 %copy-start.10 = (f32[128]{0:T(128)S(1)}, f32[128]{0:T(128)}, u32[]{:S(2)}) copy-start(f32[128]{0:T(128)} %param.23) | copy-start | bytes 1540
  0.0 1.9 %copy-start.2 = (bf16[4,64,128]{2,1,0:T(8,128)(2,1)S(1)}, bf16[4,64,128]{2,1,0:T(8,128)(2,1)}, u32[]{:S(2)}) copy-start(bf16[4,64,128]{2,1,0:T(8,128)(2,1)} %param.18) | copy-start | bytes 196612
  0.0 1.9 %copy-start.3 = (bf16[128,256]{1,0:T(8,128)(2,1)S(1)}, bf16[128,256]{1,0:T(8,128)(2,1)}, u32[]{:S(2)}) copy-start(bf16[128,256]{1,0:T(8,128)(2,1)} %edge1.1) | copy-start | bytes 196612
  1.0 0.9 %copy-start.5 = (bf16[128,128]{1,0:T(8,128)(2,1)S(1)}, bf16[128,128]{1,0:T(8,128)(2,1)}, u32[]{:S(2)}) copy-start(bf16[128,128]{1,0:T(8,128)(2,1)} %gate1.1) | copy-start | bytes 98308
  1.9 1.0 %copy-start = (bf16[256,4,256]{2,1,0:T(4,128)(2,1)S(1)}, bf16[256,4,256]{2,1,0:T(4,128)(2,1)}, u32[]{:S(2)}) copy-start(bf16[256,4,256]{2,1,0:T(4,128)(2,1)} %msa_ref.1) | copy-start | bytes 1572868
  3.0 0.9 %copy-start.1 = (bf16[1024,128]{1,0:T(8,128)(2,1)S(1)}, bf16[1024,128]{1,0:T(8,128)(2,1)}, u32[]{:S(2)}) copy-start(bf16[1024,128]{1,0:T(8,128)(2,1)} %outer_w.1) | copy-start | bytes 786436
  3.9 0.8 %copy-start.4 = (bf16[128,256]{1,0:T(8,128)(2,1)S(1)}, bf16[128,256]{1,0:T(8,128)(2,1)}, u32[]{:S(2)}) copy-start(bf16[128,256]{1,0:T(8,128)(2,1)} %edge2.1) | copy-start | bytes 196612
  4.8 0.8 %copy-start.6 = (bf16[128,128]{1,0:T(8,128)(2,1)S(1)}, bf16[128,128]{1,0:T(8,128)(2,1)}, u32[]{:S(2)}) copy-start(bf16[128,128]{1,0:T(8,128)(2,1)} %gate2.1) | copy-start | bytes 98308
  5.5 0.7 %copy-start.7 = (bf16[64,128]{1,0:T(8,128)(2,1)S(1)}, bf16[64,128]{1,0:T(8,128)(2,1)}, u32[]{:S(2)}) copy-start(bf16[64,128]{1,0:T(8,128)(2,1)} %out1.1) | copy-start | bytes 49156
  6.2 0.7 %copy-start.8 = (bf16[64,128]{1,0:T(8,128)(2,1)S(1)}, bf16[64,128]{1,0:T(8,128)(2,1)}, u32[]{:S(2)}) copy-start(bf16[64,128]{1,0:T(8,128)(2,1)} %out2.1) | copy-start | bytes 49156

commit v4 on v3

--- a/solution.py
+++ b/solution.py
@@ -157,8 +157,23 @@
     return (pair + gating * update).astype(jnp.bfloat16)
 
 
-def kernel(
-    samples,
+def kernel(samples, *refs):
+    count = (len(refs) - 23) // 2
+    operands, o_ref, held, scratch = (
+        refs[:count], refs[count], refs[count + 1 : 2 * count + 1], refs[2 * count + 1 :]
+    )
+    load_sem = scratch[-1]
+    loads = [
+        pltpu.make_async_copy(operand, here, load_sem.at[k])
+        for k, (operand, here) in enumerate(zip(operands, held))
+    ]
+    for load in loads:
+        load.start()
+    body(samples, loads, *held, o_ref, *scratch[:-1])
+
+
+def body(
+    samples, loads,
     msa_ref, msa_gain, former, latter, pair_ref, outer_w, outer_b,
     gain1, edge1, gate1, mid1, out1,
     gain2, edge2, gate2, mid2, out2,
@@ -196,24 +211,28 @@
     to_blocks = selection(
         256, lambda r: field(r, 6, 3, 2) + field(r, 4, 3, 4) + field(r, 2, 3, 0) + field(r, 0, 3, 6)
     )
+    loads[4].wait()
     psend[...] = dot(to_blocks, pair_ref[...]).astype(jnp.bfloat16).reshape(4, 64, 128)
     pbuf[m] = psend[m]
 
+    for load in loads[:4]:
+        load.wait()
     msa_scr[...] = msa_ref[...].astype(jnp.float32)
-    weights = jnp.concatenate([former[...]] * 4 + [latter[...]] * 4, axis=1)
-    position = (lax.broadcasted_iota(jnp.int32, weights.shape, 1) >> 5) & 3
+    weights = jnp.concatenate([former[...]] * 4 + [latter[...]] * 4, axis=0)
+    position = (lax.broadcasted_iota(jnp.int32, weights.shape, 0) >> 5) & 3
     factors = jnp.zeros((msa_ref.shape[0], 256), jnp.float32)
     for r in range(4):
         normed = layer_normalize(msa_scr[:, r, :], msa_gain[...]).astype(jnp.bfloat16)
         own = jnp.where(position == r, weights.astype(jnp.float32), 0.0).astype(jnp.bfloat16)
-        factors += dot(normed, own)
+        factors += lax.dot_general(
+            normed, own, (((1,), (1,)), ((), ())), preferred_element_type=jnp.float32
+        )
     lbuf[m] = factors[:, :128].astype(jnp.bfloat16)
     rbuf[z] = factors[:, 128:].astype(jnp.bfloat16)
 
     pl.semaphore_wait(barrier, 15)
-    _ = [
-        send(rbuf.at[z], rbuf.at[z], send4.at[0, d], recv4.at[0, z], same_m(d)) for d in range(1, 4)
-    ]
+    for d in range(1, 4):
+        send(rbuf.at[z], rbuf.at[z], send4.at[0, d], recv4.at[0, z], same_m(d))
     l_copies = [
         send(lbuf.at[m], lbuf.at[m], send4.at[1, d], recv4.at[1, d], same_z(d)) for d in range(1, 4)
     ]
@@ -266,6 +285,8 @@
             )
         for k in range(4):
             y_scr[:, b * 4 + k] = (x[k] * (1.0 / samples)).astype(jnp.bfloat16).reshape(8, 16, 128)
+    for load in loads[5:]:
+        load.wait()
     update = sum(
         dot(y_scr[a].reshape(256, 128), outer_w[a * 128 : (a + 1) * 128, :]) for a in range(8)
     )
@@ -291,10 +312,10 @@
 
     def outgoing(j, carry):
         zj, rj = j // 4, j % 4
-        total = jnp.zeros((16, 128), jnp.float32)
+        parts = [jnp.zeros((16, 128), jnp.float32) for _ in range(4)]
         for k in range(32):
-            total += a_scr[k] * b_scr[zj, k // 8, pl.ds((k % 8) * 4 + rj, 1), :]
-        mixed_scr[j] = total
+            parts[k % 4] += a_scr[k] * b_scr[zj, k // 8, pl.ds((k % 8) * 4 + rj, 1), :]
+        mixed_scr[j] = (parts[0] + parts[1]) + (parts[2] + parts[3])
         return carry
 
     lax.fori_loop(0, 16, outgoing, 0, unroll=4)
@@ -327,10 +348,10 @@
 
     def incoming(j, carry):
         jb, jr = j // 4, j % 4
-        total = jnp.zeros((16, 128), jnp.float32)
+        parts = [jnp.zeros((16, 128), jnp.float32) for _ in range(4)]
         for k in range(32):
-            total += a_scr[k] * b_scr[k // 8, jb, pl.ds(jr * 8 + k % 8, 1), :]
-        mixed_scr[j] = total
+            parts[k % 4] += a_scr[k] * b_scr[k // 8, jb, pl.ds(jr * 8 + k % 8, 1), :]
+        mixed_scr[j] = (parts[0] + parts[1]) + (parts[2] + parts[3])
         return carry
 
     lax.fori_loop(0, 16, incoming, 0, unroll=4)
@@ -356,14 +377,18 @@
     embedding, pair_state, norm_scale, former, latter = args[:5]
     samples = embedding.shape[0]
     rest = [a.reshape(1, -1) if a.ndim == 1 else a for a in args[5:]]
+    operands = [
+        embedding, norm_scale.reshape(1, -1), former.T, latter.T, pair_state.reshape(256, 128), *rest
+    ]
     bf16, f32 = jnp.bfloat16, jnp.float32
     vmem = pl.BlockSpec(memory_space=pltpu.VMEM)
     out = pl.pallas_call(
         functools.partial(kernel, samples),
         out_shape=jax.ShapeDtypeStruct((4, 64, 128), bf16),
-        in_specs=[vmem] * (5 + len(rest)),
+        in_specs=[pl.BlockSpec(memory_space=pl.ANY)] * len(operands),
         out_specs=vmem,
-        scratch_shapes=[
+        scratch_shapes=[pltpu.VMEM(a.shape, a.dtype) for a in operands]
+        + [
             pltpu.VMEM(embedding.shape, f32),
             pltpu.VMEM((4, 256, 128), bf16),
             pltpu.VMEM((4, 256, 128), bf16),
@@ -385,11 +410,12 @@
             pltpu.SemaphoreType.DMA((6, 4)),
             pltpu.SemaphoreType.DMA((2, 16)),
             pltpu.SemaphoreType.DMA((2, 16)),
+            pltpu.SemaphoreType.DMA((len(operands),)),
         ],
         compiler_params=pltpu.CompilerParams(
-            collective_id=0, has_side_effects=True, vmem_limit_bytes=32 * 1024 * 1024
+            collective_id=0, has_side_effects=True, vmem_limit_bytes=60 * 1024 * 1024
         ),
-    )(embedding, norm_scale.reshape(1, -1), former, latter, pair_state.reshape(256, 128), *rest)
+    )(*operands)
     return out.reshape(4, 4, 4, 4, 128).transpose(1, 2, 0, 3, 4).reshape(pair_state.shape)
 
 

time: 41.4 us -> 35.7 us (0.86); the launches traced: 40.8 us -> 35.6 us
  local copies, waits for them, and re-layouts: 7.48 us -> 1.49 us
  Pallas kernels: 33.2 us -> 34.1 us
    unnamed x32 -> x0, local copies, waits for them, and re-layouts: 6.83 us -> none
    pallas_call x1, Pallas kernels: 33.2 us -> 34.1 us  [blocks(): pl.pallas_call(functools.partial(kernel, samples), out_shape=jax.ShapeDty...]
    transpose x1, local copies, waits for them, and re-layouts: 0.65 us -> 1.49 us  [blocks(): out.reshape(4, 4, 4, 4, 128).transpose(1, 2, 0, 3, 4)]
where the time goes in v4:
time: 35.7 us; the launch traced here: 35.6 us
  Pallas kernels  34.1 us (96%)
  local copies, waits for them, and re-layouts  1.49 us (4%)
    pallas_call x1, Pallas kernels, blocks(): pl.pallas_call(functools.partial(kernel, samples), out_shape=jax.ShapeDty...  34.1 us
    transpose x1, local copies, waits for them, and re-layouts, blocks(): out.reshape(4, 4, 4, 4, 128).transpose(1, 2, 0, 3, 4)  1.49 us

profile of v4, /device:TPU:0, one launch (start us, length us, event | category | flops | bytes accessed | tf_op | source)
XLA Modules:
  0.0 35.6 jit_solution(10627875069106360377)
XLA Ops:
  0.0 34.1 %shard_map.163 = bf16[4,64,128]{2,1,0:T(8,128)(2,1)} custom-call(bf16[256,4,256]{2,1,0:T(4,128)(2,1)} %refs_0_.1, f32[1,256]{1,0:T(1,128)} %bitcast.17, bf16[32,256]{1,0:T(8,128)(2,1)} %bitcast.15, bf16[32,256]{1,0:T(8,128)(2,1)} %bitcast.16, bf16[256,128]{1,0:T(8,128)(2,1)} %bitcast.14, bf16[1024,128]{1,0:T(8,128)(2,1)} %refs_5_.1, f32[1,128]{1,0:T(1,128)} %bitcast.18, ...), custom_call_target="tpu_custom_call" | custom-call | tf_op jit(solution)/shard_map/pallas_call | solution.py:385
  34.1 1.5 %copy.18 = bf16[4,4,4,4,128]{4,3,2,1,0:T(4,128)(2,1)} copy(bf16[4,4,4,4,128]{4,3,1,0,2:T(4,128)(2,1)} %bitcast.13) | data formatting | bytes 131072 | tf_op jit(solution)/shard_map/transpose | solution.py:419

commit v5 on v4

--- a/solution.py
+++ b/solution.py
@@ -328,17 +328,19 @@
     b2buf[z] = b_half
     a2buf[z, m] = a2send[z]
     a2_copies = [
-        send(
-            a2send.at[((me + d) % 16) // 4], a2buf.at[z, m], send16.at[1, d], recv16.at[1, d],
-            (me + d) % 16,
-        )
-        for d in range(1, 16)
+        send(a2send.at[(z + d) % 4], a2buf.at[z, m], send4.at[6, d], recv4.at[6, d], same_m(d))
+        for d in range(1, 4)
     ]
     b2_copies = [
         send(b2buf.at[z], b2buf.at[z], send4.at[4, d], recv4.at[4, d], same_m(d)) for d in range(1, 4)
     ]
     by_step = selection(128, lambda r: field(r, 2, 3, 5) + field(r, 0, 3, 3) + field(r, 4, 7, 0))
     for copy in a2_copies:
+        copy.wait_recv()
+    for copy in [
+        send(a2buf.at[:, m], a2buf.at[:, m], send4.at[7, d], recv4.at[7, d], same_z(d))
+        for d in range(1, 4)
+    ]:
         copy.wait_recv()
     for k in range(4):
         a_scr[k * 8 : (k + 1) * 8] = dot(by_step, a2buf[k].reshape(128, 128)).reshape(8, 16, 128)
@@ -406,10 +408,10 @@
             pltpu.VMEM((4, 128, 128), bf16),
             pltpu.VMEM((4, 64, 128), bf16),
             pltpu.VMEM((4, 64, 128), bf16),
-            pltpu.SemaphoreType.DMA((6, 4)),
-            pltpu.SemaphoreType.DMA((6, 4)),
-            pltpu.SemaphoreType.DMA((2, 16)),
-            pltpu.SemaphoreType.DMA((2, 16)),
+            pltpu.SemaphoreType.DMA((8, 4)),
+            pltpu.SemaphoreType.DMA((8, 4)),
+            pltpu.SemaphoreType.DMA((1, 16)),
+            pltpu.SemaphoreType.DMA((1, 16)),
             pltpu.SemaphoreType.DMA((len(operands),)),
         ],
         compiler_params=pltpu.CompilerParams(

time: 35.7 us -> 34.7 us (0.972)
  Pallas kernels: 34.1 us -> 33 us
    pallas_call x1, Pallas kernels: 34.1 us -> 33 us  [blocks(): pl.pallas_call(functools.partial(kernel, samples), out_shape=jax.ShapeDty...]
where the time goes in v5:
time: 34.7 us; the launch traced here: 34.5 us
  Pallas kernels  33 us (95%)
  local copies, waits for them, and re-layouts  1.49 us (4%)
    pallas_call x1, Pallas kernels, blocks(): pl.pallas_call(functools.partial(kernel, samples), out_shape=jax.ShapeDty...  33 us
    transpose x1, local copies, waits for them, and re-layouts, blocks(): out.reshape(4, 4, 4, 4, 128).transpose(1, 2, 0, 3, 4)  1.49 us

profile of v5, /device:TPU:0, one launch (start us, length us, event | category | flops | bytes accessed | tf_op | source)
XLA Modules:
  0.0 34.5 jit_solution(10736332258631397691)
XLA Ops:
  0.0 33.0 %shard_map.163 = bf16[4,64,128]{2,1,0:T(8,128)(2,1)} custom-call(bf16[256,4,256]{2,1,0:T(4,128)(2,1)} %refs_0_.1, f32[1,256]{1,0:T(1,128)} %bitcast.17, bf16[32,256]{1,0:T(8,128)(2,1)} %bitcast.15, bf16[32,256]{1,0:T(8,128)(2,1)} %bitcast.16, bf16[256,128]{1,0:T(8,128)(2,1)} %bitcast.14, bf16[1024,128]{1,0:T(8,128)(2,1)} %refs_5_.1, f32[1,128]{1,0:T(1,128)} %bitcast.18, ...), custom_call_target="tpu_custom_call" | custom-call | tf_op jit(solution)/shard_map/pallas_call | solution.py:387
  33.0 1.5 %copy.18 = bf16[4,4,4,4,128]{4,3,2,1,0:T(4,128)(2,1)} copy(bf16[4,4,4,4,128]{4,3,1,0,2:T(4,128)(2,1)} %bitcast.13) | data formatting | bytes 131072 | tf_op jit(solution)/shard_map/transpose | solution.py:421
